TPU v7x, 256 devices: a whole 4x4x8 slice. The times are simulated.
256 devices in a mesh: slab: 16 (over y, x), gx: 16 (over z, core).
Axes of the slice: x: 4, y: 4, z: 8, core: 2. Of those that a mesh axis runs over, the one named last changes fastest.
Arguments:
- wavefield: bfloat16 [16, 2, 2048, 2048], P('slab', None, 'gx'), may hold values from -6 to 6
- boundary: bfloat16 [16, 2, 2048, 2048], P('slab', None, 'gx'), may hold values from -6 to 6
- source: bfloat16 [16, 2, 2048, 2048], P('slab', None, 'gx'), may hold values from -6 to 6
- slowness: float32 [16, 2048, 2048], P('slab', 'gx'), may hold values from 0.6 to 1.4
- reflectivity: float32 [16, 2048, 2048], P('slab', 'gx'), may hold values from -0.6 to 0.6
- ref_slowness: float32 [16], P('slab'), may hold values from 0.8 to 1.2
Outputs:
- extrapolated: bfloat16 [16, 2, 2048, 2048], P('slab', None, 'gx')
- image: float32 [16, 2048, 2048], P('slab', 'gx')
All inputs are finite; a program needn't handle non-finite values.
Results may differ from a plain program's by a relative error of at most 0.001.
Values may be sent and summed in bfloat16 or wider, within the bound.
A program may use at most 64 MiB of HBM per device.

v0:
```python
import functools
import math

import jax
import jax.numpy as jnp
from jax import lax
from jax.experimental import pallas as pl
from jax.experimental.pallas import tpu as pltpu
from jax.sharding import PartitionSpec as P
import ml_dtypes
import numpy as np

OMEGA = 2.5
DEPTH_STEP = 1.0
RADIX = 16
INNER = 128
LENGTH = RADIX * INNER
STEP = 16
PARTS = INNER // STEP
TOP = 236.0
FLOOR = 2.0**-7.8
f32 = jnp.float32
bf16 = jnp.bfloat16


def dft_tables():
    k = np.arange(RADIX)[:, None, None]
    m = np.arange(INNER)[None, :, None]
    b = np.arange(INNER)[None, None, :]
    angle = 2.0 * np.pi * ((b * (k + RADIX * m)) % LENGTH) / LENGTH
    cosine, sine = np.cos(angle), np.sin(angle)
    forward = np.concatenate(
        [np.concatenate([cosine, sine], axis=2), np.concatenate([-sine, cosine], axis=2)], axis=1
    )
    tables = []
    for table in (forward, np.swapaxes(forward, 1, 2)):
        high = table.astype(ml_dtypes.bfloat16)
        low = (table - high.astype(np.float64)).astype(ml_dtypes.bfloat16)
        tables.append(np.concatenate([high, low], axis=1))
    return tables


def rotate(value, eighth, sign):
    re, im = value
    eighth %= 16
    if eighth == 0:
        return value
    if eighth == 4:
        return (-im, re) if sign > 0 else (im, -re)
    c, s = math.cos(math.pi * eighth / 8), sign * math.sin(math.pi * eighth / 8)
    if eighth == 2:
        return ((re - im) * c, (re + im) * c) if sign > 0 else ((re + im) * c, (im - re) * c)
    if eighth == 6:
        return ((re + im) * c, (im - re) * c) if sign > 0 else ((re - im) * c, (re + im) * c)
    return (re * c - im * s, im * c + re * s)


def four(a, b, c, d, sign):
    t0 = (a[0] + c[0], a[1] + c[1])
    t1 = (a[0] - c[0], a[1] - c[1])
    t2 = (b[0] + d[0], b[1] + d[1])
    u = (b[0] - d[0], b[1] - d[1])
    t3 = (-u[1], u[0]) if sign > 0 else (u[1], -u[0])
    return (
        (t0[0] + t2[0], t0[1] + t2[1]),
        (t1[0] + t3[0], t1[1] + t3[1]),
        (t0[0] - t2[0], t0[1] - t2[1]),
        (t1[0] - t3[0], t1[1] - t3[1]),
    )


def sixteen(values, sign):
    first = [four(values[j], values[4 + j], values[8 + j], values[12 + j], sign) for j in range(4)]
    out = [None] * 16
    for k in range(4):
        column = four(*(rotate(first[j][k], j * k, sign) for j in range(4)), sign)
        for q in range(4):
            out[k + 4 * q] = column[q]
    return out


def encode(value, factor):
    w = jnp.abs(value) * factor + FLOOR
    w = w * w
    w = w * w
    w = w * w
    w = w * w
    return jnp.where(value < 0.0, -w, w).astype(bf16)


def decode(code, factor):
    v = code.astype(f32)
    w = (jnp.exp(jnp.log(jnp.abs(v)) * (1.0 / 16.0)) - FLOOR) * factor
    return jnp.where(v < 0.0, -w, w)


def split(value):
    high = value.astype(bf16)
    return high, (value - high.astype(f32)).astype(bf16)


def mm(a, b):
    return jnp.dot(a, b, preferred_element_type=f32)


def rows(start, size):
    return pl.ds(pl.multiple_of(start, size), size)


def kernel(
    wave_h, bound_h, src_h, slow_h, refl_h, base_s, fwd_h, inv_h,
    ext_h, img_h,
    wave, bound, src, slow, refl, fwd, inv,
    own, handed, lensed, mixed, snd1, rcv1, snd2, rcv2,
    tile_hi, tile_lo, tile, yhi, ylo, prop, xhi, xlo, work, ext, img,
    hmax_s, hmax_r, sc1_s, sc1_r, sc2_s, sc2_r,
    load_sem, hs_sem, hr_sem, s1_sem, r1_sem, s2_sem, r2_sem, out_sem, tiny_s, tiny_r,
):
    me = lax.axis_index("gx")
    slab = lax.axis_index("slab")
    slabs = lax.axis_size("slab")
    above = lax.rem(slab + slabs - 1, slabs)
    below = lax.rem(slab + 1, slabs)
    base = base_s[0]

    loads = [
        pltpu.make_async_copy(a, b, load_sem.at[i])
        for i, (a, b) in enumerate(
            [(bound_h.at[0], bound), (src_h.at[0], src), (refl_h.at[0], refl), (wave_h.at[0], wave),
             (slow_h.at[0], slow), (inv_h, inv), (fwd_h, fwd)]
        )
    ]
    for load in loads:
        load.start()

    barrier = pltpu.get_barrier_semaphore()

    @pl.loop(1, RADIX)
    def _(o):
        pl.semaphore_signal(barrier, inc=1, device_id={"gx": lax.rem(me + o, RADIX)}, device_id_type=pl.DeviceIdType.MESH)

    pl.semaphore_signal(barrier, inc=1, device_id={"slab": below}, device_id_type=pl.DeviceIdType.MESH)
    pl.semaphore_wait(barrier, RADIX)

    def hand_copy(c):
        return pltpu.make_async_remote_copy(
            src_ref=bound.at[:, rows(c * STEP, STEP)],
            dst_ref=handed.at[c],
            send_sem=hs_sem.at[c],
            recv_sem=hr_sem.at[c],
            device_id={"slab": above},
            device_id_type=pl.DeviceIdType.MESH,
        )

    def tiny_copy(src_ref, dst_ref, i, where):
        return pltpu.make_async_remote_copy(
            src_ref=src_ref, dst_ref=dst_ref, send_sem=tiny_s.at[i], recv_sem=tiny_r.at[i],
            device_id=where, device_id_type=pl.DeviceIdType.MESH,
        )

    loads[0].wait()

    @pl.loop(0, PARTS)
    def _(c):
        hand_copy(c).start()

    def bound_max(i, peak):
        v = jnp.abs(bound[:, rows(i * 16, 16), :].astype(f32))
        return jnp.maximum(peak, jnp.max(v.reshape(4, 8, LENGTH), axis=0))

    peak = lax.fori_loop(0, PARTS, bound_max, jnp.zeros((8, LENGTH), f32))
    hmax_s[...] = jnp.broadcast_to(jnp.max(peak, axis=(0, 1), keepdims=True), (1, INNER))
    hmax_copy = tiny_copy(hmax_s, hmax_r, 0, {"slab": above})
    hmax_copy.start()

    loads[1].wait()
    loads[2].wait()
    loads[3].wait()

    def own_part(i, peak):
        at = rows(i * 16, 16)
        scaled = refl[at, :] * (OMEGA * OMEGA)
        for p in range(2):
            v = wave[p, at, :].astype(f32) + scaled * src[p, at, :].astype(f32)
            own[p, at, :] = v
            peak = jnp.maximum(peak, jnp.max(jnp.abs(v).reshape(2, 8, LENGTH), axis=0))
        return peak

    peak = lax.fori_loop(0, PARTS, own_part, jnp.zeros((8, LENGTH), f32))
    hmax_copy.wait()
    top = jnp.broadcast_to(jnp.max(peak, axis=(0, 1), keepdims=True), (1, INNER)) + hmax_r[...]
    limit1 = jnp.maximum(top * (16.0 * 1.4143), 1e-30)

    def announce(store, gather, limit, i):
        store[...] = limit
        gather[me] = limit

        @pl.loop(1, RADIX)
        def _(o):
            tiny_copy(store, gather.at[me], i, {"gx": lax.rem(me + o, RADIX)}).start()

    def heard(gather, i):
        fifteen = gather.at[pl.ds(0, RADIX - 1)]
        pltpu.make_async_copy(fifteen, fifteen, tiny_r.at[i]).wait()
        pltpu.make_async_copy(fifteen, fifteen, tiny_s.at[i]).wait()

    announce(sc1_s, sc1_r, limit1, 1)
    factor1 = TOP / limit1
    loads[4].wait()
    loads[5].wait()
    loads[6].wait()

    def send_all(c, snd, rcv, s_sem, r_sem):
        rcv[c, me] = snd[c, me]

        @pl.loop(1, RADIX)
        def _(o):
            to = lax.rem(me + o, RADIX)
            pltpu.make_async_remote_copy(
                src_ref=snd.at[c, to], dst_ref=rcv.at[c, me], send_sem=s_sem.at[c], recv_sem=r_sem.at[c],
                device_id={"gx": to}, device_id_type=pl.DeviceIdType.MESH,
            ).start()

    def arrived(c, rcv, r_sem):
        fifteen = rcv.at[c, pl.ds(0, RADIX - 1)]
        pltpu.make_async_copy(fifteen, fifteen, r_sem.at[c]).wait()

    def first_half(c):
        at = rows(c * STEP, STEP)
        pltpu.make_async_copy(handed.at[c], handed.at[c], hr_sem.at[c]).wait()
        keep = (slab < slabs - 1).astype(f32)

        @pl.loop(0, 4)
        def _(j):
            cols = rows(j * 512, 512)
            angle = (slow[at, cols] - base) * (-OMEGA * DEPTH_STEP)
            cosine, sine = jnp.cos(angle), jnp.sin(angle)
            re = own[0, at, cols] + handed[c, 0, :, cols].astype(f32) * keep
            im = own[1, at, cols] + handed[c, 1, :, cols].astype(f32) * keep
            lensed[0, :, cols] = re * cosine - im * sine
            lensed[1, :, cols] = re * sine + im * cosine

        for g in range(STEP // 8):
            group = pl.ds(g * 8, 8)
            cells = [
                tuple(lensed[p, group, pl.ds(y * INNER, INNER)] for p in range(2)) for y in range(RADIX)
            ]
            for d, cell in enumerate(sixteen(cells, -1)):
                for p in range(2):
                    mixed[d, p, group, :] = cell[p]

        @pl.loop(0, 4)
        def _(j):
            four_at = rows(j * 4, 4)
            snd1[c, four_at] = encode(mixed[four_at], factor1.reshape(1, 1, 1, INNER))

        send_all(c, snd1, rcv1, s1_sem, r1_sem)

    def propagator(k):
        kx = k + RADIX * lax.broadcasted_iota(jnp.int32, (INNER, INNER), 0)
        ky = me + RADIX * lax.broadcasted_iota(jnp.int32, (INNER, INNER), 1)
        fx = jnp.where(kx < LENGTH // 2, kx, kx - LENGTH).astype(f32) * (2.0 * math.pi / LENGTH)
        fy = jnp.where(ky < LENGTH // 2, ky, ky - LENGTH).astype(f32) * (2.0 * math.pi / LENGTH)
        kz2 = (OMEGA * base) * (OMEGA * base) - fx * fx - fy * fy
        root = jnp.sqrt(jnp.abs(kz2))
        upward = kz2 >= 0.0
        scale = 1.0 / (LENGTH * LENGTH)
        prop[k, 0] = jnp.where(upward, jnp.cos(root * DEPTH_STEP), jnp.exp(-root * DEPTH_STEP)) * scale
        prop[k, 1] = jnp.where(upward, -jnp.sin(root * DEPTH_STEP), 0.0) * scale

    def times_table(table):
        high, low = table[me, pl.ds(0, 256)], table[me, pl.ds(256, 256)]
        a, b = tile_hi[...], tile_lo[...]
        tile[...] = mm(a, high) + (mm(b, high) + mm(a, low))

    def second_half(c):
        arrived(c, rcv1, r1_sem)

        @pl.loop(0, 4)
        def _(j):
            four_at = rows(j * 4, 4)
            factor = sc1_r[four_at].reshape(4, 1, 1, INNER) * (1.0 / TOP)
            value = decode(rcv1[c, four_at], factor)
            for p in range(2):
                high, low = split(value[:, p].reshape(4 * STEP, INNER))
                tile_hi[rows(j * 64, 64), pl.ds(p * INNER, INNER)] = high
                tile_lo[rows(j * 64, 64), pl.ds(p * INNER, INNER)] = low

        times_table(inv)
        for g in range(STEP // 8):
            cells = [
                tuple(tile[pl.ds(a * STEP + g * 8, 8), pl.ds(p * INNER, INNER)] for p in range(2)) for a in range(RADIX)
            ]
            for k, cell in enumerate(sixteen(cells, -1)):
                for p in range(2):
                    mixed[k, p, pl.ds(g * 8, 8), :] = cell[p]

        for p in range(2):
            high, low = split(mixed[:, p])
            at = rows(p * INNER + c * STEP, STEP)
            yhi[:, at, :] = high
            ylo[:, at, :] = low

    @pl.loop(0, PARTS)
    def _(c):
        first_half(c)

        @pl.loop(0, RADIX // PARTS)
        def _(j):
            propagator(c * (RADIX // PARTS) + j)

        @pl.when(c == 1)
        def _():
            heard(sc1_r, 1)

        @pl.when(c > 0)
        def _():
            second_half(c - 1)

    second_half(PARTS - 1)

    def along_x(table, k, high, low):
        both = mm(table[k], high)
        return both[:256] + (both[256:] + mm(table[k, pl.ds(0, 256)], low))

    def middle(k, energy):
        spectrum = along_x(fwd, k, yhi[k], ylo[k])
        re, im = spectrum[:INNER], spectrum[INNER:]
        pr, pi = prop[k, 0], prop[k, 1]
        out_re = re * pr - im * pi
        out_im = re * pi + im * pr
        energy = energy + jnp.sum((out_re * out_re + out_im * out_im).reshape(16, 8, INNER), axis=0)
        hr, lr = split(out_re)
        hi, li = split(out_im)
        xhi[pl.ds(0, INNER)] = hr
        xhi[pl.ds(INNER, INNER)] = hi
        xlo[pl.ds(0, INNER)] = lr
        xlo[pl.ds(INNER, INNER)] = li
        work[k] = along_x(inv, k, xhi[...], xlo[...])
        return energy

    energy = lax.fori_loop(0, RADIX, middle, jnp.zeros((8, INNER), f32))
    total = jnp.broadcast_to(jnp.sum(energy, axis=(0, 1), keepdims=True), (1, INNER))
    limit2 = jnp.maximum(jnp.sqrt(total) * 513.0, 1e-30)
    announce(sc2_s, sc2_r, limit2, 2)
    factor2 = TOP / limit2

    def third_half(c):
        for g in range(STEP // 8):
            cells = [
                tuple(work[k, rows(p * INNER + c * STEP + g * 8, 8), :] for p in range(2)) for k in range(RADIX)
            ]
            for a, cell in enumerate(sixteen(cells, 1)):
                for p in range(2):
                    tile[pl.ds(a * STEP + g * 8, 8), pl.ds(p * INNER, INNER)] = cell[p]

        @pl.loop(0, 4)
        def _(j):
            at = rows(j * 64, 64)
            high, low = split(tile[at, :])
            tile_hi[at, :] = high
            tile_lo[at, :] = low

        times_table(fwd)

        @pl.loop(0, 4)
        def _(j):
            code = encode(tile[rows(j * 64, 64), :].reshape(4, STEP, 256), jnp.concatenate([factor2, factor2], axis=1).reshape(1, 1, 256))
            for p in range(2):
                snd2[c, rows(j * 4, 4), p] = code[:, :, p * INNER:(p + 1) * INNER]

        send_all(c, snd2, rcv2, s2_sem, r2_sem)

    def outputs(c):
        at = rows(c * STEP, STEP)
        return (
            pltpu.make_async_copy(ext.at[:, at], ext_h.at[0, :, at], out_sem.at[0, c]),
            pltpu.make_async_copy(img.at[at], img_h.at[0, at], out_sem.at[1, c]),
        )

    def fourth_half(c):
        arrived(c, rcv2, r2_sem)

        @pl.loop(0, 4)
        def _(j):
            four_at = rows(j * 4, 4)
            factor = sc2_r[four_at].reshape(4, 1, 1, INNER) * (1.0 / TOP)
            mixed[four_at] = decode(rcv2[c, four_at], factor)

        for g in range(STEP // 8):
            group = pl.ds(g * 8, 8)
            cells = [tuple(mixed[d, p, group, :] for p in range(2)) for d in range(RADIX)]
            for y, cell in enumerate(sixteen(cells, 1)):
                for p in range(2):
                    lensed[p, group, pl.ds(y * INNER, INNER)] = cell[p]

        at = rows(c * STEP, STEP)

        @pl.loop(0, 4)
        def _(j):
            cols = rows(j * 512, 512)
            re, im = lensed[0, :, cols], lensed[1, :, cols]
            ext[0, at, cols] = re.astype(bf16)
            ext[1, at, cols] = im.astype(bf16)
            img[at, cols] = src[0, at, cols].astype(f32) * re + src[1, at, cols].astype(f32) * im

        for copy in outputs(c):
            copy.start()

    @pl.loop(0, PARTS)
    def _(c):
        third_half(c)

        @pl.when(c == 1)
        def _():
            heard(sc2_r, 2)

        @pl.when(c > 0)
        def _():
            fourth_half(c - 1)

    fourth_half(PARTS - 1)

    @pl.loop(0, PARTS)
    def _(c):
        for copy in outputs(c):
            copy.wait()
        pltpu.make_async_copy(handed.at[c], handed.at[c], hs_sem.at[c]).wait()
        for snd, sem in ((snd1, s1_sem), (snd2, s2_sem)):
            fifteen = snd.at[c, pl.ds(0, RADIX - 1)]
            pltpu.make_async_copy(fifteen, fifteen, sem.at[c]).wait()


def body(wavefield, boundary, source, slowness, reflectivity, ref_slowness, forward, inverse):
    anywhere = pl.BlockSpec(memory_space=pl.ANY)
    field = (2, INNER, LENGTH)
    block = (PARTS, RADIX, 2, STEP, INNER)
    vmem = pltpu.VMEM
    return pl.pallas_call(
        kernel,
        out_shape=(
            jax.ShapeDtypeStruct((1,) + field, bf16),
            jax.ShapeDtypeStruct((1, INNER, LENGTH), f32),
        ),
        in_specs=[anywhere] * 5 + [pl.BlockSpec(memory_space=pltpu.SMEM)] + [anywhere] * 2,
        out_specs=(anywhere, anywhere),
        scratch_shapes=[
            vmem(field, bf16), vmem(field, bf16), vmem(field, bf16), vmem(field[1:], f32), vmem(field[1:], f32),
            vmem((RADIX, 512, 256), bf16), vmem((RADIX, 512, 256), bf16),
            vmem(field, f32), vmem((PARTS, 2, STEP, LENGTH), bf16), vmem((2, STEP, LENGTH), f32), vmem(block[1:], f32),
            vmem(block, bf16), vmem(block, bf16), vmem(block, bf16), vmem(block, bf16),
            vmem((256, 256), bf16), vmem((256, 256), bf16), vmem((256, 256), f32),
            vmem((RADIX, 256, INNER), bf16), vmem((RADIX, 256, INNER), bf16), vmem((RADIX, 2, INNER, INNER), f32),
            vmem((256, INNER), bf16), vmem((256, INNER), bf16), vmem((RADIX, 256, INNER), f32),
            vmem(field, bf16), vmem(field[1:], f32),
            vmem((1, INNER), f32), vmem((1, INNER), f32),
            vmem((1, INNER), f32), vmem((RADIX, 1, INNER), f32), vmem((1, INNER), f32), vmem((RADIX, 1, INNER), f32),
            pltpu.SemaphoreType.DMA((7,)),
            pltpu.SemaphoreType.DMA((PARTS,)), pltpu.SemaphoreType.DMA((PARTS,)),
            pltpu.SemaphoreType.DMA((PARTS,)), pltpu.SemaphoreType.DMA((PARTS,)),
            pltpu.SemaphoreType.DMA((PARTS,)), pltpu.SemaphoreType.DMA((PARTS,)),
            pltpu.SemaphoreType.DMA((2, PARTS)),
            pltpu.SemaphoreType.DMA((3,)), pltpu.SemaphoreType.DMA((3,)),
        ],
        compiler_params=pltpu.CompilerParams(
            collective_id=0, has_side_effects=True, vmem_limit_bytes=56 * 1024 * 1024
        ),
    )(wavefield, boundary, source, slowness, reflectivity, ref_slowness, forward, inverse)


def solution(mesh):
    forward, inverse = dft_tables()
    step = jax.shard_map(
        body,
        mesh=mesh,
        in_specs=(
            P("slab", None, "gx", None),
            P("slab", None, "gx", None),
            P("slab", None, "gx", None),
            P("slab", "gx", None),
            P("slab", "gx", None),
            P("slab"),
            P(),
            P(),
        ),
        out_specs=(P("slab", None, "gx", None), P("slab", "gx", None)),
        check_vma=False,
    )

    def whole(wavefield, boundary, source, slowness, reflectivity, ref_slowness):
        return step(
            wavefield, boundary, source, slowness, reflectivity, ref_slowness, jnp.asarray(forward), jnp.asarray(inverse)
        )

    return whole
```

profile of v0, /device:TPU:1, one launch (start us, length us, event | category | flops | bytes accessed | tf_op | source)
XLA Modules:
  0.0 117.0 jit_solution(6379135394096577973)
XLA Ops:
  1.3 111.1 %shard_map.95 = (bf16[1,2,128,2048]{3,2,1,0:T(8,128)(2,1)}, f32[1,128,2048]{2,1,0:T(8,128)}) custom-call(bf16[1,2,128,2048]{3,2,1,0:T(8,128)(2,1)} %wave_h.1, bf16[1,2,128,2048]{3,2,1,0:T(8,128)(2,1)} %bound_h.1, bf16[1,2,128,2048]{3,2,1,0:T(8,128)(2,1)} %src_h.1, f32[1,128,2048]{2,1,0:T(8,128)} %slow_h.1, f32[1,128,2048]{2,1,0:T(8,128)} %refl_h.1, ...), custom_call_target="tpu_custom_call" | custom-call | tf_op jit(solution)/shard_map/pallas_call | solution.py:439
  112.4 2.3 %copy.13 = bf16[1,2,128,2048]{3,2,1,0:T(8,128)(2,1)} copy(bf16[1,2,128,2048]{3,2,1,0:T(8,128)(2,1)} %get-tuple-element.4) | data formatting | bytes 2097152
  114.7 2.3 %copy.14 = f32[1,128,2048]{2,1,0:T(8,128)} copy(f32[1,128,2048]{2,1,0:T(8,128)} %get-tuple-element.5) | data formatting | bytes 2097152
where the time goes:
time: 118 us; the launch traced here: 117 us
  Pallas kernels  111 us (94%)
  local copies, waits for them, and re-layouts  4.6 us (4%)
  between operations  1.29 us (1%)
    pallas_call x1, Pallas kernels, body(): pl.pallas_call(kernel, out_shape=(jax.ShapeDtypeStruct((1,) + field, bf16...  111 us
    unnamed x2, local copies, waits for them, and re-layouts  4.6 us

commit v1 on v0

--- a/solution.py
+++ b/solution.py
@@ -17,6 +17,9 @@
 LENGTH = RADIX * INNER
 STEP = 16
 PARTS = INNER // STEP
+AHEAD = 2
+LAG = 2
+FAR_FIRST = (4, 3, 5, 2, 6, 1, 7, 0)
 TOP = 236.0
 FLOOR = 2.0**-7.8
 f32 = jnp.float32
@@ -130,9 +133,6 @@
              (slow_h.at[0], slow), (inv_h, inv), (fwd_h, fwd)]
         )
     ]
-    for load in loads:
-        load.start()
-
     barrier = pltpu.get_barrier_semaphore()
 
     @pl.loop(1, RADIX)
@@ -140,11 +140,13 @@
         pl.semaphore_signal(barrier, inc=1, device_id={"gx": lax.rem(me + o, RADIX)}, device_id_type=pl.DeviceIdType.MESH)
 
     pl.semaphore_signal(barrier, inc=1, device_id={"slab": below}, device_id_type=pl.DeviceIdType.MESH)
+    for load in loads:
+        load.start()
     pl.semaphore_wait(barrier, RADIX)
 
     def hand_copy(c):
         return pltpu.make_async_remote_copy(
-            src_ref=bound.at[:, rows(c * STEP, STEP)],
+            src_ref=bound_h.at[0, :, rows(c * STEP, STEP)],
             dst_ref=handed.at[c],
             send_sem=hs_sem.at[c],
             recv_sem=hr_sem.at[c],
@@ -158,11 +160,10 @@
             device_id=where, device_id_type=pl.DeviceIdType.MESH,
         )
 
+    for c in range(AHEAD):
+        hand_copy(c).start()
+
     loads[0].wait()
-
-    @pl.loop(0, PARTS)
-    def _(c):
-        hand_copy(c).start()
 
     def bound_max(i, peak):
         v = jnp.abs(bound[:, rows(i * 16, 16), :].astype(f32))
@@ -213,13 +214,14 @@
     def send_all(c, snd, rcv, s_sem, r_sem):
         rcv[c, me] = snd[c, me]
 
-        @pl.loop(1, RADIX)
-        def _(o):
-            to = lax.rem(me + o, RADIX)
-            pltpu.make_async_remote_copy(
-                src_ref=snd.at[c, to], dst_ref=rcv.at[c, me], send_sem=s_sem.at[c], recv_sem=r_sem.at[c],
-                device_id={"gx": to}, device_id_type=pl.DeviceIdType.MESH,
-            ).start()
+        for hop in FAR_FIRST:
+            for other in range(2):
+                if hop or other:
+                    to = lax.rem(me // 2 + hop, RADIX // 2) * 2 + lax.rem(me + other, 2)
+                    pltpu.make_async_remote_copy(
+                        src_ref=snd.at[c, to], dst_ref=rcv.at[c, me], send_sem=s_sem.at[c], recv_sem=r_sem.at[c],
+                        device_id={"gx": to}, device_id_type=pl.DeviceIdType.MESH,
+                    ).start()
 
     def arrived(c, rcv, r_sem):
         fifteen = rcv.at[c, pl.ds(0, RADIX - 1)]
@@ -227,7 +229,12 @@
 
     def first_half(c):
         at = rows(c * STEP, STEP)
-        pltpu.make_async_copy(handed.at[c], handed.at[c], hr_sem.at[c]).wait()
+        hand_copy(c).wait()
+
+        @pl.when(c < PARTS - AHEAD)
+        def _():
+            hand_copy(c + AHEAD).start()
+
         keep = (slab < slabs - 1).astype(f32)
 
         @pl.loop(0, 4)
@@ -309,15 +316,17 @@
         def _(j):
             propagator(c * (RADIX // PARTS) + j)
 
-        @pl.when(c == 1)
+        @pl.when(c == LAG)
         def _():
             heard(sc1_r, 1)
 
-        @pl.when(c > 0)
+        @pl.when(c >= LAG)
         def _():
-            second_half(c - 1)
-
-    second_half(PARTS - 1)
+            second_half(c - LAG)
+
+    @pl.loop(PARTS - LAG, PARTS)
+    def _(c):
+        second_half(c)
 
     def along_x(table, k, high, low):
         both = mm(table[k], high)
@@ -411,21 +420,22 @@
     def _(c):
         third_half(c)
 
-        @pl.when(c == 1)
+        @pl.when(c == LAG)
         def _():
             heard(sc2_r, 2)
 
-        @pl.when(c > 0)
+        @pl.when(c >= LAG)
         def _():
-            fourth_half(c - 1)
-
-    fourth_half(PARTS - 1)
+            fourth_half(c - LAG)
+
+    @pl.loop(PARTS - LAG, PARTS)
+    def _(c):
+        fourth_half(c)
 
     @pl.loop(0, PARTS)
     def _(c):
         for copy in outputs(c):
             copy.wait()
-        pltpu.make_async_copy(handed.at[c], handed.at[c], hs_sem.at[c]).wait()
         for snd, sem in ((snd1, s1_sem), (snd2, s2_sem)):
             fifteen = snd.at[c, pl.ds(0, RADIX - 1)]
             pltpu.make_async_copy(fifteen, fifteen, sem.at[c]).wait()

time: 118 us -> 86.8 us (0.74)
  Pallas kernels: 111 us -> 80.8 us
    pallas_call x1, Pallas kernels: 111 us -> 80.8 us  [body(): pl.pallas_call(kernel, out_shape=(jax.ShapeDtypeStruct((1,) + field, bf16...]
where the time goes in v1:
time: 86.8 us; the launch traced here: 86.6 us
  Pallas kernels  80.8 us (93%)
  local copies, waits for them, and re-layouts  4.6 us (5%)
  between operations  1.29 us (1%)
    pallas_call x1, Pallas kernels, body(): pl.pallas_call(kernel, out_shape=(jax.ShapeDtypeStruct((1,) + field, bf16...  80.8 us
    unnamed x2, local copies, waits for them, and re-layouts  4.6 us

profile of v1, /device:TPU:1, one launch (start us, length us, event | category | flops | bytes accessed | tf_op | source)
XLA Modules:
  0.0 86.6 jit_solution(4566066447607746534)
XLA Ops:
  1.3 80.8 %shard_map.95 = (bf16[1,2,128,2048]{3,2,1,0:T(8,128)(2,1)}, f32[1,128,2048]{2,1,0:T(8,128)}) custom-call(bf16[1,2,128,2048]{3,2,1,0:T(8,128)(2,1)} %wave_h.1, bf16[1,2,128,2048]{3,2,1,0:T(8,128)(2,1)} %bound_h.1, bf16[1,2,128,2048]{3,2,1,0:T(8,128)(2,1)} %src_h.1, f32[1,128,2048]{2,1,0:T(8,128)} %slow_h.1, f32[1,128,2048]{2,1,0:T(8,128)} %refl_h.1, ...), custom_call_target="tpu_custom_call" | custom-call | tf_op jit(solution)/shard_map/pallas_call | solution.py:449
  82.0 2.3 %copy.13 = bf16[1,2,128,2048]{3,2,1,0:T(8,128)(2,1)} copy(bf16[1,2,128,2048]{3,2,1,0:T(8,128)(2,1)} %get-tuple-element.4) | data formatting | bytes 2097152
  84.3 2.3 %copy.14 = f32[1,128,2048]{2,1,0:T(8,128)} copy(f32[1,128,2048]{2,1,0:T(8,128)} %get-tuple-element.5) | data formatting | bytes 2097152

commit v2 on v1

--- a/solution.py
+++ b/solution.py
@@ -18,7 +18,9 @@
 STEP = 16
 PARTS = INNER // STEP
 AHEAD = 2
-LAG = 2
+HALF = PARTS // 2
+LAG = 3
+GROUP = 4
 FAR_FIRST = (4, 3, 5, 2, 6, 1, 7, 0)
 TOP = 236.0
 FLOOR = 2.0**-7.8
@@ -40,6 +42,10 @@
         high = table.astype(ml_dtypes.bfloat16)
         low = (table - high.astype(np.float64)).astype(ml_dtypes.bfloat16)
         tables.append(np.concatenate([high, low], axis=1))
+    tables.append(tables[1][0].reshape(2, 2, 2, 64, 256).swapaxes(1, 2).reshape(512, 256))
+    turn = 2.0 * np.pi * (k[:, :, 0] * b[0]) / LENGTH
+    turn = np.stack([np.cos(turn), np.sin(turn)], axis=1).astype(np.float32)
+    tables.append(np.broadcast_to(turn[..., None], (RADIX, 2, INNER, INNER)))
     return tables
 
 
@@ -111,12 +117,12 @@
 
 
 def kernel(
-    wave_h, bound_h, src_h, slow_h, refl_h, base_s, fwd_h, inv_h,
+    wave_h, bound_h, src_h, slow_h, refl_h, base_h, fwd_h, inv_h, inv0_h, turn_h,
     ext_h, img_h,
-    wave, bound, src, slow, refl, fwd, inv,
+    wave, bound, src, slow, refl, fwd, inv, fwd0, inv0, turn,
     own, handed, lensed, mixed, snd1, rcv1, snd2, rcv2,
-    tile_hi, tile_lo, tile, yhi, ylo, prop, xhi, xlo, work, ext, img,
-    hmax_s, hmax_r, sc1_s, sc1_r, sc2_s, sc2_r,
+    tile_hi, tile_lo, tile, yhi, ylo, xhi, xlo, prop, work, ext, img,
+    base_s, hmax_s, hmax_r, sc1_s, sc1_r, sc2_s, sc2_r,
     load_sem, hs_sem, hr_sem, s1_sem, r1_sem, s2_sem, r2_sem, out_sem, tiny_s, tiny_r,
 ):
     me = lax.axis_index("gx")
@@ -124,13 +130,11 @@
     slabs = lax.axis_size("slab")
     above = lax.rem(slab + slabs - 1, slabs)
     below = lax.rem(slab + 1, slabs)
-    base = base_s[0]
-
     loads = [
         pltpu.make_async_copy(a, b, load_sem.at[i])
         for i, (a, b) in enumerate(
             [(bound_h.at[0], bound), (src_h.at[0], src), (refl_h.at[0], refl), (wave_h.at[0], wave),
-             (slow_h.at[0], slow), (inv_h, inv), (fwd_h, fwd)]
+             (slow_h.at[0], slow), (inv_h.at[me], inv), (fwd_h.at[me], fwd), (inv0_h, inv0), (fwd_h.at[0], fwd0), (turn_h, turn), (base_h, base_s)]
         )
     ]
     barrier = pltpu.get_barrier_semaphore()
@@ -160,9 +164,7 @@
             device_id=where, device_id_type=pl.DeviceIdType.MESH,
         )
 
-    for c in range(AHEAD):
-        hand_copy(c).start()
-
+    hand_copy(0).start()
     loads[0].wait()
 
     def bound_max(i, peak):
@@ -173,6 +175,8 @@
     hmax_s[...] = jnp.broadcast_to(jnp.max(peak, axis=(0, 1), keepdims=True), (1, INNER))
     hmax_copy = tiny_copy(hmax_s, hmax_r, 0, {"slab": above})
     hmax_copy.start()
+    hand_copy(0).wait_send()
+    hand_copy(1).start()
 
     loads[1].wait()
     loads[2].wait()
@@ -207,9 +211,9 @@
 
     announce(sc1_s, sc1_r, limit1, 1)
     factor1 = TOP / limit1
-    loads[4].wait()
-    loads[5].wait()
-    loads[6].wait()
+    for load in loads[4:]:
+        load.wait()
+    base = base_s[0]
 
     def send_all(c, snd, rcv, s_sem, r_sem):
         rcv[c, me] = snd[c, me]
@@ -229,7 +233,11 @@
 
     def first_half(c):
         at = rows(c * STEP, STEP)
-        hand_copy(c).wait()
+        hand_copy(c).wait_recv()
+
+        @pl.when(c > 0)
+        def _():
+            hand_copy(c).wait_send()
 
         @pl.when(c < PARTS - AHEAD)
         def _():
@@ -272,11 +280,12 @@
         root = jnp.sqrt(jnp.abs(kz2))
         upward = kz2 >= 0.0
         scale = 1.0 / (LENGTH * LENGTH)
-        prop[k, 0] = jnp.where(upward, jnp.cos(root * DEPTH_STEP), jnp.exp(-root * DEPTH_STEP)) * scale
-        prop[k, 1] = jnp.where(upward, -jnp.sin(root * DEPTH_STEP), 0.0) * scale
+        pair, lanes = k // 2, rows(k % 2 * INNER, INNER)
+        prop[pair, 0, :, lanes] = jnp.where(upward, jnp.cos(root * DEPTH_STEP), jnp.exp(-root * DEPTH_STEP)) * scale
+        prop[pair, 1, :, lanes] = jnp.where(upward, -jnp.sin(root * DEPTH_STEP), 0.0) * scale
 
     def times_table(table):
-        high, low = table[me, pl.ds(0, 256)], table[me, pl.ds(256, 256)]
+        high, low = table[pl.ds(0, 256)], table[pl.ds(256, 256)]
         a, b = tile_hi[...], tile_lo[...]
         tile[...] = mm(a, high) + (mm(b, high) + mm(a, low))
 
@@ -298,15 +307,19 @@
             cells = [
                 tuple(tile[pl.ds(a * STEP + g * 8, 8), pl.ds(p * INNER, INNER)] for p in range(2)) for a in range(RADIX)
             ]
-            for k, cell in enumerate(sixteen(cells, -1)):
-                for p in range(2):
-                    mixed[k, p, pl.ds(g * 8, 8), :] = cell[p]
-
-        for p in range(2):
-            high, low = split(mixed[:, p])
-            at = rows(p * INNER + c * STEP, STEP)
-            yhi[:, at, :] = high
-            ylo[:, at, :] = low
+            for k, (re, im) in enumerate(sixteen(cells, -1)):
+                if k:
+                    cosine, sine = (turn[k, p, rows(c * STEP + g * 8, 8), :] for p in range(2))
+                    re, im = re * cosine + im * sine, im * cosine - re * sine
+                mixed[k, 0, pl.ds(g * 8, 8), :] = re
+                mixed[k, 1, pl.ds(g * 8, 8), :] = im
+
+        for k in range(RADIX):
+            for p in range(2):
+                high, low = split(mixed[k, p])
+                at = rows(p * INNER + c * STEP, STEP)
+                yhi[k // 2, at, pl.ds(k % 2 * INNER, INNER)] = high
+                ylo[k // 2, at, pl.ds(k % 2 * INNER, INNER)] = low
 
     @pl.loop(0, PARTS)
     def _(c):
@@ -328,37 +341,50 @@
     def _(c):
         second_half(c)
 
-    def along_x(table, k, high, low):
-        both = mm(table[k], high)
-        return both[:256] + (both[256:] + mm(table[k, pl.ds(0, 256)], low))
-
-    def middle(k, energy):
-        spectrum = along_x(fwd, k, yhi[k], ylo[k])
+    def along_x(table, start, count, high, low):
+        coarse, fine = table[pl.ds(start, count)], table[pl.ds(256 + start, count)]
+        return mm(coarse, high) + (mm(fine, high) + mm(coarse, low))
+
+    def forward_x(k):
+        spectrum = along_x(fwd0, 0, 256, yhi[k], ylo[k])
         re, im = spectrum[:INNER], spectrum[INNER:]
         pr, pi = prop[k, 0], prop[k, 1]
         out_re = re * pr - im * pi
         out_im = re * pi + im * pr
-        energy = energy + jnp.sum((out_re * out_re + out_im * out_im).reshape(16, 8, INNER), axis=0)
-        hr, lr = split(out_re)
-        hi, li = split(out_im)
-        xhi[pl.ds(0, INNER)] = hr
-        xhi[pl.ds(INNER, INNER)] = hi
-        xlo[pl.ds(0, INNER)] = lr
-        xlo[pl.ds(INNER, INNER)] = li
-        work[k] = along_x(inv, k, xhi[...], xlo[...])
+        for p, value in enumerate((out_re, out_im)):
+            high, low = split(value)
+            xhi[k, pl.ds(p * INNER, INNER)] = high
+            xlo[k, pl.ds(p * INNER, INNER)] = low
+        return jnp.sum((out_re * out_re + out_im * out_im).reshape(16, 8, 256), axis=0)
+
+    def forwards(i, energy):
+        for k in range(GROUP):
+            energy = energy + forward_x(i * GROUP + k)
         return energy
 
-    energy = lax.fori_loop(0, RADIX, middle, jnp.zeros((8, INNER), f32))
+    def inverse_x(half):
+        @pl.loop(0, RADIX // 2 // GROUP)
+        def _(i):
+            for k in range(GROUP):
+                k = i * GROUP + k
+                work[k, pl.ds(half * INNER, INNER)] = along_x(inv0, half * INNER, INNER, xhi[k], xlo[k])
+
+    energy = lax.fori_loop(0, RADIX // 2 // GROUP, forwards, jnp.zeros((8, 256), f32))
     total = jnp.broadcast_to(jnp.sum(energy, axis=(0, 1), keepdims=True), (1, INNER))
     limit2 = jnp.maximum(jnp.sqrt(total) * 513.0, 1e-30)
     announce(sc2_s, sc2_r, limit2, 2)
     factor2 = TOP / limit2
+    inverse_x(0)
 
     def third_half(c):
         for g in range(STEP // 8):
-            cells = [
-                tuple(work[k, rows(p * INNER + c * STEP + g * 8, 8), :] for p in range(2)) for k in range(RADIX)
-            ]
+            cells = []
+            for k in range(RADIX):
+                re, im = (work[k // 2, rows(c // HALF * INNER + p * 64 + c % HALF * STEP + g * 8, 8), pl.ds(k % 2 * INNER, INNER)] for p in range(2))
+                if k:
+                    cosine, sine = (turn[k, p, rows(c * STEP + g * 8, 8), :] for p in range(2))
+                    re, im = re * cosine - im * sine, im * cosine + re * sine
+                cells.append((re, im))
             for a, cell in enumerate(sixteen(cells, 1)):
                 for p in range(2):
                     tile[pl.ds(a * STEP + g * 8, 8), pl.ds(p * INNER, INNER)] = cell[p]
@@ -419,6 +445,10 @@
     @pl.loop(0, PARTS)
     def _(c):
         third_half(c)
+
+        @pl.when(c == HALF - 1)
+        def _():
+            inverse_x(1)
 
         @pl.when(c == LAG)
         def _():
@@ -441,31 +471,49 @@
             pltpu.make_async_copy(fifteen, fifteen, sem.at[c]).wait()
 
 
-def body(wavefield, boundary, source, slowness, reflectivity, ref_slowness, forward, inverse):
+def deliver(ext_h, img_h, ext_o, img_o, ext, img, sem):
+    def copies(j):
+        at = pl.ds(j * 32, 32)
+        return (
+            (ext_h.at[0, :, at], ext.at[:, at], ext_o.at[0, :, at], sem.at[0, j], sem.at[1, j]),
+            (img_h.at[0, at], img.at[at], img_o.at[0, at], sem.at[2, j], sem.at[3, j]),
+        )
+
+    every = [copy for j in range(4) for copy in copies(j)]
+    for a, b, _, come, _ in every:
+        pltpu.make_async_copy(a, b, come).start()
+    for a, b, out, come, go in every:
+        pltpu.make_async_copy(a, b, come).wait()
+        pltpu.make_async_copy(b, out, go).start()
+    for _, b, out, _, go in every:
+        pltpu.make_async_copy(b, out, go).wait()
+
+
+def body(wavefield, boundary, source, slowness, reflectivity, ref_slowness, forward, inverse, inverse0, turn):
     anywhere = pl.BlockSpec(memory_space=pl.ANY)
     field = (2, INNER, LENGTH)
     block = (PARTS, RADIX, 2, STEP, INNER)
     vmem = pltpu.VMEM
-    return pl.pallas_call(
+    shapes = (jax.ShapeDtypeStruct((1,) + field, bf16), jax.ShapeDtypeStruct((1, INNER, LENGTH), f32))
+    results = pl.pallas_call(
         kernel,
-        out_shape=(
-            jax.ShapeDtypeStruct((1,) + field, bf16),
-            jax.ShapeDtypeStruct((1, INNER, LENGTH), f32),
-        ),
-        in_specs=[anywhere] * 5 + [pl.BlockSpec(memory_space=pltpu.SMEM)] + [anywhere] * 2,
+        out_shape=shapes,
+        in_specs=[anywhere] * 10,
         out_specs=(anywhere, anywhere),
         scratch_shapes=[
             vmem(field, bf16), vmem(field, bf16), vmem(field, bf16), vmem(field[1:], f32), vmem(field[1:], f32),
-            vmem((RADIX, 512, 256), bf16), vmem((RADIX, 512, 256), bf16),
+            vmem((512, 256), bf16), vmem((512, 256), bf16), vmem((512, 256), bf16), vmem((512, 256), bf16),
+            vmem((RADIX, 2, INNER, INNER), f32),
             vmem(field, f32), vmem((PARTS, 2, STEP, LENGTH), bf16), vmem((2, STEP, LENGTH), f32), vmem(block[1:], f32),
             vmem(block, bf16), vmem(block, bf16), vmem(block, bf16), vmem(block, bf16),
             vmem((256, 256), bf16), vmem((256, 256), bf16), vmem((256, 256), f32),
-            vmem((RADIX, 256, INNER), bf16), vmem((RADIX, 256, INNER), bf16), vmem((RADIX, 2, INNER, INNER), f32),
-            vmem((256, INNER), bf16), vmem((256, INNER), bf16), vmem((RADIX, 256, INNER), f32),
+            vmem((RADIX // 2, 256, 256), bf16), vmem((RADIX // 2, 256, 256), bf16),
+            vmem((RADIX // 2, 256, 256), bf16), vmem((RADIX // 2, 256, 256), bf16), vmem((RADIX // 2, 2, INNER, 256), f32),
+            vmem((RADIX // 2, 256, 256), f32),
             vmem(field, bf16), vmem(field[1:], f32),
-            vmem((1, INNER), f32), vmem((1, INNER), f32),
+            pltpu.SMEM((1,), f32), vmem((1, INNER), f32), vmem((1, INNER), f32),
             vmem((1, INNER), f32), vmem((RADIX, 1, INNER), f32), vmem((1, INNER), f32), vmem((RADIX, 1, INNER), f32),
-            pltpu.SemaphoreType.DMA((7,)),
+            pltpu.SemaphoreType.DMA((11,)),
             pltpu.SemaphoreType.DMA((PARTS,)), pltpu.SemaphoreType.DMA((PARTS,)),
             pltpu.SemaphoreType.DMA((PARTS,)), pltpu.SemaphoreType.DMA((PARTS,)),
             pltpu.SemaphoreType.DMA((PARTS,)), pltpu.SemaphoreType.DMA((PARTS,)),
@@ -475,11 +523,18 @@
         compiler_params=pltpu.CompilerParams(
             collective_id=0, has_side_effects=True, vmem_limit_bytes=56 * 1024 * 1024
         ),
-    )(wavefield, boundary, source, slowness, reflectivity, ref_slowness, forward, inverse)
+    )(wavefield, boundary, source, slowness, reflectivity, ref_slowness, forward, inverse, inverse0, turn)
+    return pl.pallas_call(
+        deliver,
+        out_shape=shapes,
+        in_specs=[anywhere] * 2,
+        out_specs=(anywhere, anywhere),
+        scratch_shapes=[vmem(field, bf16), vmem(field[1:], f32), pltpu.SemaphoreType.DMA((4, 4))],
+    )(*results)
 
 
 def solution(mesh):
-    forward, inverse = dft_tables()
+    forward, inverse, inverse0, turn = dft_tables()
     step = jax.shard_map(
         body,
         mesh=mesh,
@@ -492,6 +547,8 @@
             P("slab"),
             P(),
             P(),
+            P(),
+            P(),
         ),
         out_specs=(P("slab", None, "gx", None), P("slab", "gx", None)),
         check_vma=False,
@@ -499,7 +556,8 @@
 
     def whole(wavefield, boundary, source, slowness, reflectivity, ref_slowness):
         return step(
-            wavefield, boundary, source, slowness, reflectivity, ref_slowness, jnp.asarray(forward), jnp.asarray(inverse)
+            wavefield, boundary, source, slowness, reflectivity, ref_slowness,
+            jnp.asarray(forward), jnp.asarray(inverse), jnp.asarray(inverse0), jnp.asarray(turn),
         )
 
     return whole

time: 86.8 us -> 76.9 us (0.89)
  Pallas kernels: 80.8 us -> 72.8 us
  local copies, waits for them, and re-layouts: 4.6 us -> 2.67 us
    pallas_call x1 -> x2, Pallas kernels: 80.8 us -> 72.8 us  [the longest x1 70.4 us: body(): pl.pallas_call(kernel, out_shape=shapes, in_specs=[anywhere] * 10, out_sp...]
    unnamed x2 -> x0, local copies, waits for them, and re-layouts: 4.6 us -> none
    another operation x0 -> x1, local copies, waits for them, and re-layouts: none -> 2.67 us
where the time goes in v2:
time: 76.9 us; the launch traced here: 76.7 us
  Pallas kernels  72.8 us (95%)
  local copies, waits for them, and re-layouts  2.67 us (3%)
  between operations  1.28 us (2%)
    pallas_call x1, Pallas kernels, body(): pl.pallas_call(kernel, out_shape=shapes, in_specs=[anywhere] * 10, out_sp...  70.4 us
    another operation x1, local copies, waits for them, and re-layouts  2.67 us
    pallas_call x1, Pallas kernels, body(): pl.pallas_call(deliver, out_shape=shapes, in_specs=[anywhere] * 2, out_sp...  2.4 us

profile of v2, /device:TPU:1, one launch (start us, length us, event | category | flops | bytes accessed | tf_op | source)
XLA Modules:
  0.0 76.7 jit_solution(8851016443251563527)
XLA Ops:
  1.3 2.7 %jit_solution_.3.turn_h = f32[16,2,128,128]{3,2,1,0:T(8,128)} broadcast(f32[16,2,128]{2,1,0:T(2,128)} %constant.11.clone), dimensions={0,1,2} | broadcast | bytes 2113536 | tf_op jit(solution)
  3.9 70.4 %shard_map.113 = (bf16[1,2,128,2048]{3,2,1,0:T(8,128)(2,1)}, f32[1,128,2048]{2,1,0:T(8,128)}) custom-call(bf16[1,2,128,2048]{3,2,1,0:T(8,128)(2,1)} %wave_h.1, bf16[1,2,128,2048]{3,2,1,0:T(8,128)(2,1)} %bound_h.1, bf16[1,2,128,2048]{3,2,1,0:T(8,128)(2,1)} %src_h.1, f32[1,128,2048]{2,1,0:T(8,128)} %slow_h.1, f32[1,128,2048]{2,1,0:T(8,128)} %refl_h.1, ...), custom_call_target="tpu_custom_call" | custom-call | tf_op jit(solution)/shard_map/pallas_call | solution.py:498
  74.3 2.4 %shard_map.114 = (bf16[1,2,128,2048]{3,2,1,0:T(8,128)(2,1)}, f32[1,128,2048]{2,1,0:T(8,128)}) custom-call(bf16[1,2,128,2048]{3,2,1,0:T(8,128)(2,1)} %get-tuple-element.4.ext_h, f32[1,128,2048]{2,1,0:T(8,128)} %get-tuple-element.5.img_h), custom_call_target="tpu_custom_call" | custom-call | tf_op jit(solution)/shard_map/pallas_call | solution.py:527

commit v3 on v2

--- a/solution.py
+++ b/solution.py
@@ -20,7 +20,7 @@
 AHEAD = 2
 HALF = PARTS // 2
 LAG = 3
-GROUP = 4
+GROUP = 8
 FAR_FIRST = (4, 3, 5, 2, 6, 1, 7, 0)
 TOP = 236.0
 FLOOR = 2.0**-7.8
@@ -245,7 +245,7 @@
 
         keep = (slab < slabs - 1).astype(f32)
 
-        @pl.loop(0, 4)
+        @pl.loop(0, 4, unroll=True)
         def _(j):
             cols = rows(j * 512, 512)
             angle = (slow[at, cols] - base) * (-OMEGA * DEPTH_STEP)
@@ -264,7 +264,7 @@
                 for p in range(2):
                     mixed[d, p, group, :] = cell[p]
 
-        @pl.loop(0, 4)
+        @pl.loop(0, 4, unroll=True)
         def _(j):
             four_at = rows(j * 4, 4)
             snd1[c, four_at] = encode(mixed[four_at], factor1.reshape(1, 1, 1, INNER))
@@ -292,7 +292,7 @@
     def second_half(c):
         arrived(c, rcv1, r1_sem)
 
-        @pl.loop(0, 4)
+        @pl.loop(0, 4, unroll=True)
         def _(j):
             four_at = rows(j * 4, 4)
             factor = sc1_r[four_at].reshape(4, 1, 1, INNER) * (1.0 / TOP)
@@ -389,7 +389,7 @@
                 for p in range(2):
                     tile[pl.ds(a * STEP + g * 8, 8), pl.ds(p * INNER, INNER)] = cell[p]
 
-        @pl.loop(0, 4)
+        @pl.loop(0, 4, unroll=True)
         def _(j):
             at = rows(j * 64, 64)
             high, low = split(tile[at, :])
@@ -398,7 +398,7 @@
 
         times_table(fwd)
 
-        @pl.loop(0, 4)
+        @pl.loop(0, 4, unroll=True)
         def _(j):
             code = encode(tile[rows(j * 64, 64), :].reshape(4, STEP, 256), jnp.concatenate([factor2, factor2], axis=1).reshape(1, 1, 256))
             for p in range(2):
@@ -416,7 +416,7 @@
     def fourth_half(c):
         arrived(c, rcv2, r2_sem)
 
-        @pl.loop(0, 4)
+        @pl.loop(0, 4, unroll=True)
         def _(j):
             four_at = rows(j * 4, 4)
             factor = sc2_r[four_at].reshape(4, 1, 1, INNER) * (1.0 / TOP)
@@ -431,7 +431,7 @@
 
         at = rows(c * STEP, STEP)
 
-        @pl.loop(0, 4)
+        @pl.loop(0, 4, unroll=True)
         def _(j):
             cols = rows(j * 512, 512)
             re, im = lensed[0, :, cols], lensed[1, :, cols]
@@ -471,22 +471,16 @@
             pltpu.make_async_copy(fifteen, fifteen, sem.at[c]).wait()
 
 
-def deliver(ext_h, img_h, ext_o, img_o, ext, img, sem):
-    def copies(j):
+def deliver(ext_h, img_h, ext_o, img_o, sem):
+    copies = []
+    for j in range(4):
         at = pl.ds(j * 32, 32)
-        return (
-            (ext_h.at[0, :, at], ext.at[:, at], ext_o.at[0, :, at], sem.at[0, j], sem.at[1, j]),
-            (img_h.at[0, at], img.at[at], img_o.at[0, at], sem.at[2, j], sem.at[3, j]),
-        )
-
-    every = [copy for j in range(4) for copy in copies(j)]
-    for a, b, _, come, _ in every:
-        pltpu.make_async_copy(a, b, come).start()
-    for a, b, out, come, go in every:
-        pltpu.make_async_copy(a, b, come).wait()
-        pltpu.make_async_copy(b, out, go).start()
-    for _, b, out, _, go in every:
-        pltpu.make_async_copy(b, out, go).wait()
+        copies.append(pltpu.make_async_copy(ext_h.at[0, :, at], ext_o.at[0, :, at], sem.at[0, j]))
+        copies.append(pltpu.make_async_copy(img_h.at[0, at], img_o.at[0, at], sem.at[1, j]))
+    for copy in copies:
+        copy.start()
+    for copy in copies:
+        copy.wait()
 
 
 def body(wavefield, boundary, source, slowness, reflectivity, ref_slowness, forward, inverse, inverse0, turn):
@@ -521,15 +515,16 @@
             pltpu.SemaphoreType.DMA((3,)), pltpu.SemaphoreType.DMA((3,)),
         ],
         compiler_params=pltpu.CompilerParams(
-            collective_id=0, has_side_effects=True, vmem_limit_bytes=56 * 1024 * 1024
+            collective_id=0, has_side_effects=True, vmem_limit_bytes=44 * 1024 * 1024
         ),
-    )(wavefield, boundary, source, slowness, reflectivity, ref_slowness, forward, inverse, inverse0, turn)
+    )(*(x if x is ref_slowness else pltpu.with_memory_space_constraint(x, pltpu.HBM) for x in (wavefield, boundary, source, slowness, reflectivity, ref_slowness, forward, inverse, inverse0, turn)))
     return pl.pallas_call(
         deliver,
         out_shape=shapes,
         in_specs=[anywhere] * 2,
         out_specs=(anywhere, anywhere),
-        scratch_shapes=[vmem(field, bf16), vmem(field[1:], f32), pltpu.SemaphoreType.DMA((4, 4))],
+        scratch_shapes=[pltpu.SemaphoreType.DMA((2, 4))],
+        compiler_params=pltpu.CompilerParams(vmem_limit_bytes=4 * 1024 * 1024),
     )(*results)
 
 

time: 76.9 us -> 74.6 us (0.970)
  Pallas kernels: 72.8 us -> 70.5 us
    pallas_call x1, Pallas kernels: 70.4 us -> 69.1 us  [body(): pl.pallas_call(kernel, out_shape=shapes, in_specs=[anywhere] * 10, out_sp...]
    pallas_call x1, Pallas kernels: 2.4 us -> 1.38 us  [body(): pl.pallas_call(deliver, out_shape=shapes, in_specs=[anywhere] * 2, out_sp...]
where the time goes in v3:
time: 74.6 us; the launch traced here: 74.4 us
  Pallas kernels  70.5 us (95%)
  local copies, waits for them, and re-layouts  2.67 us (4%)
  between operations  1.28 us (2%)
    pallas_call x1, Pallas kernels, body(): pl.pallas_call(kernel, out_shape=shapes, in_specs=[anywhere] * 10, out_sp...  69.1 us
    another operation x1, local copies, waits for them, and re-layouts  2.67 us

profile of v3, /device:TPU:1, one launch (start us, length us, event | category | flops | bytes accessed | tf_op | source)
XLA Modules:
  0.0 74.4 jit_solution(10198324340965180371)
XLA Ops:
  1.3 2.7 %jit_solution_.3.turn_h = f32[16,2,128,128]{3,2,1,0:T(8,128)} broadcast(f32[16,2,128]{2,1,0:T(2,128)} %constant.11.clone), dimensions={0,1,2} | broadcast | bytes 2113536 | tf_op jit(solution)
  3.9 69.1 %shard_map.113 = (bf16[1,2,128,2048]{3,2,1,0:T(8,128)(2,1)S(1)}, f32[1,128,2048]{2,1,0:T(8,128)S(1)}) custom-call(bf16[1,2,128,2048]{3,2,1,0:T(8,128)(2,1)} %wave_h.1, bf16[1,2,128,2048]{3,2,1,0:T(8,128)(2,1)} %bound_h.1, bf16[1,2,128,2048]{3,2,1,0:T(8,128)(2,1)} %src_h.1, f32[1,128,2048]{2,1,0:T(8,128)} %slow_h.1, f32[1,128,2048]{2,1,0:T(8,128)} %refl_h.1, ...), custom_call_target="tpu_custom_call" | custom-call | tf_op jit(solution)/shard_map/pallas_call | solution.py:492
  73.1 1.4 %shard_map.114 = (bf16[1,2,128,2048]{3,2,1,0:T(8,128)(2,1)}, f32[1,128,2048]{2,1,0:T(8,128)}) custom-call(bf16[1,2,128,2048]{3,2,1,0:T(8,128)(2,1)S(1)} %get-tuple-element.4.ext_h, f32[1,128,2048]{2,1,0:T(8,128)S(1)} %get-tuple-element.5.img_h), custom_call_target="tpu_custom_call" | custom-call | tf_op jit(solution)/shard_map/pallas_call | solution.py:521

commit v4 on v3

--- a/solution.py
+++ b/solution.py
@@ -17,7 +17,7 @@
 LENGTH = RADIX * INNER
 STEP = 16
 PARTS = INNER // STEP
-AHEAD = 2
+AHEAD = 3
 HALF = PARTS // 2
 LAG = 3
 GROUP = 8
@@ -192,6 +192,7 @@
         return peak
 
     peak = lax.fori_loop(0, PARTS, own_part, jnp.zeros((8, LENGTH), f32))
+    hand_copy(2).start()
     hmax_copy.wait()
     top = jnp.broadcast_to(jnp.max(peak, axis=(0, 1), keepdims=True), (1, INNER)) + hmax_r[...]
     limit1 = jnp.maximum(top * (16.0 * 1.4143), 1e-30)

time: 74.6 us -> 74.9 us (level)
  no operation moved by 1% of the time
where the time goes in v4:
time: 74.9 us; the launch traced here: 74.8 us
  Pallas kernels  70.8 us (95%)
  local copies, waits for them, and re-layouts  2.67 us (4%)
  between operations  1.28 us (2%)
    pallas_call x1, Pallas kernels, body(): pl.pallas_call(kernel, out_shape=shapes, in_specs=[anywhere] * 10, out_sp...  69.4 us
    another operation x1, local copies, waits for them, and re-layouts  2.67 us

profile of v4, /device:TPU:1, one launch (start us, length us, event | category | flops | bytes accessed | tf_op | source)
XLA Modules:
  0.0 74.8 jit_solution(2265645991121372992)
XLA Ops:
  1.3 2.7 %jit_solution_.3.turn_h = f32[16,2,128,128]{3,2,1,0:T(8,128)} broadcast(f32[16,2,128]{2,1,0:T(2,128)} %constant.11.clone), dimensions={0,1,2} | broadcast | bytes 2113536 | tf_op jit(solution)
  3.9 69.4 %shard_map.113 = (bf16[1,2,128,2048]{3,2,1,0:T(8,128)(2,1)S(1)}, f32[1,128,2048]{2,1,0:T(8,128)S(1)}) custom-call(bf16[1,2,128,2048]{3,2,1,0:T(8,128)(2,1)} %wave_h.1, bf16[1,2,128,2048]{3,2,1,0:T(8,128)(2,1)} %bound_h.1, bf16[1,2,128,2048]{3,2,1,0:T(8,128)(2,1)} %src_h.1, f32[1,128,2048]{2,1,0:T(8,128)} %slow_h.1, f32[1,128,2048]{2,1,0:T(8,128)} %refl_h.1, ...), custom_call_target="tpu_custom_call" | custom-call | tf_op jit(solution)/shard_map/pallas_call | solution.py:493
  73.4 1.4 %shard_map.114 = (bf16[1,2,128,2048]{3,2,1,0:T(8,128)(2,1)}, f32[1,128,2048]{2,1,0:T(8,128)}) custom-call(bf16[1,2,128,2048]{3,2,1,0:T(8,128)(2,1)S(1)} %get-tuple-element.4.ext_h, f32[1,128,2048]{2,1,0:T(8,128)S(1)} %get-tuple-element.5.img_h), custom_call_target="tpu_custom_call" | custom-call | tf_op jit(solution)/shard_map/pallas_call | solution.py:522

commit v5 on v4

--- a/solution.py
+++ b/solution.py
@@ -120,7 +120,7 @@
     wave_h, bound_h, src_h, slow_h, refl_h, base_h, fwd_h, inv_h, inv0_h, turn_h,
     ext_h, img_h,
     wave, bound, src, slow, refl, fwd, inv, fwd0, inv0, turn,
-    own, handed, lensed, mixed, snd1, rcv1, snd2, rcv2,
+    own, handed, lens, lensed, mixed, snd1, rcv1, snd2, rcv2,
     tile_hi, tile_lo, tile, yhi, ylo, xhi, xlo, prop, work, ext, img,
     base_s, hmax_s, hmax_r, sc1_s, sc1_r, sc2_s, sc2_r,
     load_sem, hs_sem, hr_sem, s1_sem, r1_sem, s2_sem, r2_sem, out_sem, tiny_s, tiny_r,
@@ -234,23 +234,30 @@
 
     def first_half(c):
         at = rows(c * STEP, STEP)
-        hand_copy(c).wait_recv()
-
-        @pl.when(c > 0)
-        def _():
-            hand_copy(c).wait_send()
-
-        @pl.when(c < PARTS - AHEAD)
-        def _():
-            hand_copy(c + AHEAD).start()
-
-        keep = (slab < slabs - 1).astype(f32)
 
         @pl.loop(0, 4, unroll=True)
         def _(j):
             cols = rows(j * 512, 512)
             angle = (slow[at, cols] - base) * (-OMEGA * DEPTH_STEP)
-            cosine, sine = jnp.cos(angle), jnp.sin(angle)
+            lens[0, :, cols] = jnp.cos(angle)
+            lens[1, :, cols] = jnp.sin(angle)
+
+        hand_copy(c).wait_recv()
+
+        @pl.when(c > 0)
+        def _():
+            hand_copy(c).wait_send()
+
+        @pl.when(c < PARTS - AHEAD)
+        def _():
+            hand_copy(c + AHEAD).start()
+
+        keep = (slab < slabs - 1).astype(f32)
+
+        @pl.loop(0, 4, unroll=True)
+        def _(j):
+            cols = rows(j * 512, 512)
+            cosine, sine = lens[0, :, cols], lens[1, :, cols]
             re = own[0, at, cols] + handed[c, 0, :, cols].astype(f32) * keep
             im = own[1, at, cols] + handed[c, 1, :, cols].astype(f32) * keep
             lensed[0, :, cols] = re * cosine - im * sine
@@ -499,7 +506,7 @@
             vmem(field, bf16), vmem(field, bf16), vmem(field, bf16), vmem(field[1:], f32), vmem(field[1:], f32),
             vmem((512, 256), bf16), vmem((512, 256), bf16), vmem((512, 256), bf16), vmem((512, 256), bf16),
             vmem((RADIX, 2, INNER, INNER), f32),
-            vmem(field, f32), vmem((PARTS, 2, STEP, LENGTH), bf16), vmem((2, STEP, LENGTH), f32), vmem(block[1:], f32),
+            vmem(field, f32), vmem((PARTS, 2, STEP, LENGTH), bf16), vmem((2, STEP, LENGTH), f32), vmem((2, STEP, LENGTH), f32), vmem(block[1:], f32),
             vmem(block, bf16), vmem(block, bf16), vmem(block, bf16), vmem(block, bf16),
             vmem((256, 256), bf16), vmem((256, 256), bf16), vmem((256, 256), f32),
             vmem((RADIX // 2, 256, 256), bf16), vmem((RADIX // 2, 256, 256), bf16),

time: 74.9 us -> 74.6 us (level)
  no operation moved by 1% of the time
where the time goes in v5:
time: 74.6 us; the launch traced here: 74.5 us
  Pallas kernels  70.5 us (95%)
  local copies, waits for them, and re-layouts  2.67 us (4%)
  between operations  1.28 us (2%)
    pallas_call x1, Pallas kernels, body(): pl.pallas_call(kernel, out_shape=shapes, in_specs=[anywhere] * 10, out_sp...  69.1 us
    another operation x1, local copies, waits for them, and re-layouts  2.67 us

profile of v5, /device:TPU:1, one launch (start us, length us, event | category | flops | bytes accessed | tf_op | source)
XLA Modules:
  0.0 74.5 jit_solution(4286838504893857958)
XLA Ops:
  1.3 2.7 %jit_solution_.3.turn_h = f32[16,2,128,128]{3,2,1,0:T(8,128)} broadcast(f32[16,2,128]{2,1,0:T(2,128)} %constant.11.clone), dimensions={0,1,2} | broadcast | bytes 2113536 | tf_op jit(solution)
  3.9 69.1 %shard_map.113 = (bf16[1,2,128,2048]{3,2,1,0:T(8,128)(2,1)S(1)}, f32[1,128,2048]{2,1,0:T(8,128)S(1)}) custom-call(bf16[1,2,128,2048]{3,2,1,0:T(8,128)(2,1)} %wave_h.1, bf16[1,2,128,2048]{3,2,1,0:T(8,128)(2,1)} %bound_h.1, bf16[1,2,128,2048]{3,2,1,0:T(8,128)(2,1)} %src_h.1, f32[1,128,2048]{2,1,0:T(8,128)} %slow_h.1, f32[1,128,2048]{2,1,0:T(8,128)} %refl_h.1, ...), custom_call_target="tpu_custom_call" | custom-call | tf_op jit(solution)/shard_map/pallas_call | solution.py:500
  73.1 1.4 %shard_map.114 = (bf16[1,2,128,2048]{3,2,1,0:T(8,128)(2,1)}, f32[1,128,2048]{2,1,0:T(8,128)}) custom-call(bf16[1,2,128,2048]{3,2,1,0:T(8,128)(2,1)S(1)} %get-tuple-element.4.ext_h, f32[1,128,2048]{2,1,0:T(8,128)S(1)} %get-tuple-element.5.img_h), custom_call_target="tpu_custom_call" | custom-call | tf_op jit(solution)/shard_map/pallas_call | solution.py:529
